TPU v7x, 1024 devices: a whole 4x4x32 slice. The times are simulated.
1024 devices in a mesh: expert: 64 (over y, z_hi, x, core), replica: 16 (over z_lo).
Axes of the slice: x: 4, y: 4, z: 32 (z_hi: 2, z_lo: 16; z = z_hi * 16 + z_lo), core: 2. Of those that a mesh axis runs over, the one named last changes fastest.
Arguments:
- tokens: bfloat16 [65536, 1024], P(('expert', 'replica')), may hold values from -6 to 6
- route_ids: int32 [65536, 6], P(('expert', 'replica')), may hold values from 0 to 63, all different within a row; in each aligned block of 64 rows (0 to 63, 64 to 127, ...) at most 7 rows name the same one
- route_weights: bfloat16 [65536, 6], P(('expert', 'replica')), may hold values from 0.049804688 to 0.5
- out_grad: bfloat16 [65536, 1024], P(('expert', 'replica')), may hold values from -3 to 3
- w_gate: bfloat16 [64, 1024, 384], P('expert'), may hold values from -0.1875 to 0.1875
- w_up: bfloat16 [64, 1024, 384], P('expert'), may hold values from -0.1875 to 0.1875
- w_down: bfloat16 [64, 1024, 384], P('expert'), may hold values from -0.3125 to 0.3125
- mom_gate: float32 [64, 1024, 384], P('expert', 'replica'), may hold values from -6 to 6
- mom_up: float32 [64, 1024, 384], P('expert', 'replica'), may hold values from -6 to 6
- mom_down: float32 [64, 1024, 384], P('expert', 'replica'), may hold values from -6 to 6
Outputs:
- grad_tokens: bfloat16 [65536, 1024], P(('expert', 'replica'))
- grad_route: bfloat16 [65536, 6], P(('expert', 'replica'))
- new_gate: float32 [64, 1024, 384], P('expert', 'replica')
- new_up: float32 [64, 1024, 384], P('expert', 'replica')
- new_down: float32 [64, 1024, 384], P('expert', 'replica')
Inputs may be any that keep to these rules, and one draw needn't show every extreme that they name: `route_ids`: each row names 6 different experts. Among the 64 rows of one device no expert is named more than 7 times, a bound that some block reaches.
All inputs are finite; a program needn't handle non-finite values.
Results may differ from a plain program's by a relative error of at most 0.015.
Values may be sent and summed in bfloat16 or wider, within the bound.
A program may use at most 32 MiB of HBM per device.

v0:
```python
import math

import jax
import jax.numpy as jnp
from jax import lax
from jax.sharding import PartitionSpec as P

TOPK = 6


def in_one_piece(arrays, axis, split_dim, concat_dim, along):
    widths = [math.prod(a.shape[along:]) for a in arrays]
    both = jnp.concatenate(
        [a.reshape(*a.shape[:along], w) for a, w in zip(arrays, widths)], axis=along
    )
    filled = lax.all_to_all(both, axis, split_axis=split_dim, concat_axis=concat_dim, tiled=True)
    parts = jnp.split(filled, [sum(widths[:k]) for k in range(1, len(widths))], axis=along)
    return tuple(
        (b.reshape(*filled.shape[:along], *a.shape[along:]) for a, b in zip(arrays, parts))
    )


def slot_table(ids, experts, cap):
    flat = ids.reshape(-1)
    onehot = (flat[:, None] == jnp.arange(experts, dtype=jnp.int32)[None, :]).astype(jnp.int32)
    before = jnp.cumsum(onehot, axis=0) - onehot
    position = jnp.sum(before * onehot, axis=1)
    return flat * cap + position


def forward_pass(got_rows, w_gate, w_up, depth, width):
    rows = got_rows[:, 0].reshape(depth, width)
    gate_act = jnp.dot(rows, w_gate[0], preferred_element_type=jnp.float32)
    up_act = jnp.dot(rows, w_up[0], preferred_element_type=jnp.float32)
    sig = 1.0 / (1.0 + jnp.exp(-gate_act))
    act = gate_act * sig
    forward = [(rows, gate_act, up_act, sig, act, act * up_act)]
    return forward


def per_device(
    tokens, route_ids, route_weights, out_grad, w_gate, w_up, w_down, mom_gate, mom_up, mom_down
):
    groups = lax.axis_size("expert")
    local = w_gate.shape[0]
    experts = groups * local
    tok_rows = tokens.shape[0]
    width = tokens.shape[1]
    units = w_gate.shape[2]
    cap = 7 * tok_rows * TOPK // (6 * experts)
    depth = groups * cap
    slots = slot_table(route_ids, experts, cap)
    route_count = tok_rows * TOPK
    source = (
        jnp.zeros((experts * cap,), jnp.int32)
        .at[slots]
        .set(jnp.arange(route_count, dtype=jnp.int32) + 1)
    )
    filled = source > 0
    route_of = jnp.maximum(source - 1, 0)
    token_index = route_of // TOPK

    def pack_rows(values):
        picked_rows = jnp.where(filled[:, None], values[token_index], jnp.zeros((), values.dtype))
        return picked_rows.reshape(groups, local, cap, values.shape[1])

    packed_rows = pack_rows(tokens)
    packed_grads = pack_rows(out_grad)
    packed_weights = jnp.where(
        filled, route_weights.reshape(-1)[route_of], jnp.zeros((), route_weights.dtype)
    ).reshape(groups, local, cap)
    got_rows, got_grads, got_weights = in_one_piece(
        (packed_rows, packed_grads, packed_weights), "expert", 0, 0, 3
    )
    forward = forward_pass(got_rows, w_gate, w_up, depth, width)
    dims = (((1,), (1,)), ((), ()))
    rows, gate_act, up_act, sig, act, hidden = forward[0]
    grads = got_grads[:, 0].reshape(depth, width)
    scale = got_weights[:, 0].reshape(depth).astype(jnp.float32)[:, None]
    back = jnp.dot(grads, w_down[0], preferred_element_type=jnp.float32)
    route_list = [jnp.sum(hidden * back, axis=1).astype(jnp.bfloat16)]
    gh = scale * back
    grad_gate = (gh * up_act * sig * (1.0 + gate_act * (1.0 - sig))).astype(jnp.bfloat16)
    grad_up = (gh * act).astype(jnp.bfloat16)
    slot_grad = lax.dot_general(grad_gate, w_gate[0], dims, preferred_element_type=jnp.float32)
    slot_grad = slot_grad + lax.dot_general(
        grad_up, w_up[0], dims, preferred_element_type=jnp.float32
    )
    slot_list = [slot_grad.astype(jnp.bfloat16)]
    scaled = (scale * grads.astype(jnp.float32)).astype(jnp.bfloat16)
    send_slots = (
        jnp.stack(slot_list, axis=0).reshape(local, groups, cap, width).transpose(1, 0, 2, 3)
    )
    send_route = jnp.stack(route_list, axis=0).reshape(local, groups, cap).transpose(1, 0, 2)
    back_slots, back_route = in_one_piece((send_slots, send_route), "expert", 0, 0, 3)
    picked = back_slots.reshape(experts * cap, width)[slots].reshape(tok_rows, TOPK, width)
    grad_tokens = jnp.sum(picked.astype(jnp.float32), axis=1).astype(jnp.bfloat16)
    grad_route = back_route.reshape(experts * cap)[slots].reshape(tok_rows, TOPK)
    rdims = (((0,), (0,)), ((), ()))
    shard_rows = width // lax.axis_size("replica")
    pieces = []
    rows, grad_gate, grad_up, scaled, hidden_b = (
        rows,
        grad_gate,
        grad_up,
        scaled,
        hidden.astype(jnp.bfloat16),
    )
    pieces.append(lax.dot_general(rows, grad_gate, rdims, preferred_element_type=jnp.float32))
    pieces.append(lax.dot_general(rows, grad_up, rdims, preferred_element_type=jnp.float32))
    pieces.append(lax.dot_general(scaled, hidden_b, rdims, preferred_element_type=jnp.float32))
    summed = lax.psum_scatter(
        jnp.concatenate(pieces, axis=1).astype(jnp.bfloat16),
        "replica",
        scatter_dimension=0,
        tiled=True,
    ).astype(jnp.float32)
    summed = summed.reshape(shard_rows, local, 3, units).transpose(1, 2, 0, 3)
    new_gate = 0.9 * mom_gate + 0.1 * summed[:, 0]
    new_up = 0.9 * mom_up + 0.1 * summed[:, 1]
    new_down = 0.9 * mom_down + 0.1 * summed[:, 2]
    return (grad_tokens, grad_route, new_gate, new_up, new_down)


def solution(mesh):
    return jax.shard_map(
        per_device,
        mesh=mesh,
        in_specs=(
            P(("expert", "replica"), None),
            P(("expert", "replica"), None),
            P(("expert", "replica"), None),
            P(("expert", "replica"), None),
            P("expert", None, None),
            P("expert", None, None),
            P("expert", None, None),
            P("expert", "replica", None),
            P("expert", "replica", None),
            P("expert", "replica", None),
        ),
        out_specs=(
            P(("expert", "replica"), None),
            P(("expert", "replica"), None),
            P("expert", "replica", None),
            P("expert", "replica", None),
            P("expert", "replica", None),
        ),
        check_vma=False,
    )
```

profile of v0, /device:TPU:6, one launch (start us, length us, event | category | flops | bytes accessed | tf_op | source)
XLA Modules:
  0.0 540.8 jit_solution(12473402518307412599)
XLA Ops:
  11.6 2.9 scatter_custom_fusion
  14.5 3.2 gather_fusion.2
  18.1 2.1 gather_fusion.1
  21.2 2.7 gather_fusion
  23.9 1.4 gather.20
  25.9 106.2 %all_to_all.10 = bf16[64,1,7,2049]{3,2,1,0:T(8,128)(2,1)S(1)} all-to-all(bf16[64,1,7,2049]{3,2,1,0:T(8,128)(2,1)S(1)} %maximum_bitcast_fusion), channel_id=1, replica_groups=mesh['expert'=64,'replica'=16] {'expert'}, dimensions={0} | all-to-all | bytes 3671808 | tf_op jit(solution)/shard_map/all_to_all | solution.py:16
  132.5 1.6 fusion.28
  134.1 2.4 reshape_squeeze.7
  136.8 1.9 fusion.6
  139.4 1.8 multiply_convert_fusion.3
  141.2 0.9 convert_element_type.65
  142.8 1.6 add_convert_fusion
  144.4 1.4 transpose_reshape_stack.3
  145.8 2.2 maximum_bitcast_fusion.1
  148.0 7.8 %all-to-all-start.1 = ((bf16[64,1,7,1025]{3,2,1,0:T(8,128)(2,1)}), bf16[64,1,7,1025]{3,2,1,0:T(8,128)(2,1)}, u32[]{:S(2)}, u32[]{:S(2)}) async-start(bf16[64,1,7,1025]{3,2,1,0:T(8,128)(2,1)} %maximum_bitcast_fusion.1), calls=%async_computation.1 | async-start | bytes 2359296 | tf_op jit(solution)/shard_map/all_to_all | solution.py:16
  155.9 1.7 convolution_convert_fusion.2
  159.2 2.6 copy.36
  161.9 359.9 %reduce-scatter.4.cloned.1.call-done = bf16[64,1152]{1,0:T(8,128)(2,1)} async-done(((bf16[1024,1152]{1,0:T(8,128)(2,1)}), bf16[64,1152]{1,0:T(8,128)(2,1)}) %reduce-scatter.4.cloned.1.call-update) | async-done | bytes 147472
  521.8 1.1 copy.37
  523.8 1.3 split.23
  525.4 1.1 slice_reduce_fusion
  526.6 2.1 gather_fusion.3
  528.7 2.8 gather_fusion.4
  532.6 1.4 reduce_sum.35
  (76 shorter events, 12.3 us)
Async XLA Ops:
  7.2 132.3 %copy-start = (bf16[1,1024,384]{2,1,0:T(8,128)(2,1)S(1)}, bf16[1,1024,384]{2,1,0:T(8,128)(2,1)}, u32[]{:S(2)}) copy-start(bf16[1,1024,384]{2,1,0:T(8,128)(2,1)} %param.14) | copy-start | bytes 2359300
  7.2 11.0 %copy-start.1 = (bf16[64,1024]{1,0:T(8,128)(2,1)S(1)}, bf16[64,1024]{1,0:T(8,128)(2,1)}, u32[]{:S(2)}) copy-start(bf16[64,1024]{1,0:T(8,128)(2,1)} %param.13) | copy-start | bytes 393220
  20.3 0.9 copy-start.2
  134.1 2.4 copy-start.3
  134.1 2.7 copy-start.6
  136.8 2.0 copy-start.7
  136.8 2.6 copy-start.4
  138.8 2.4 copy-start.8
  141.2 1.6 copy-start.10
  141.2 1.6 copy-start.11
  148.0 7.9 %copy-start.5 = (bf16[448,1024]{1,0:T(8,128)(2,1)S(1)}, bf16[448,1024]{1,0:T(8,128)(2,1)}, u32[]{:S(2)}) copy-start(bf16[448,1024]{1,0:T(8,128)(2,1)} %reshape_squeeze.7) | copy-start | bytes 2752516
  148.0 375.8 %all-to-all-start.1 = ((bf16[64,1,7,1025]{3,2,1,0:T(8,128)(2,1)}), bf16[64,1,7,1025]{3,2,1,0:T(8,128)(2,1)}, u32[]{:S(2)}, u32[]{:S(2)}) async-start(bf16[64,1,7,1025]{3,2,1,0:T(8,128)(2,1)} %maximum_bitcast_fusion.1), calls=%async_computation.1 | async-start | bytes 2359296 | tf_op jit(solution)/shard_map/all_to_all | solution.py:16
  155.9 2.4 copy-start.9
  155.9 365.9 %reduce-scatter.4.cloned.1.call-start = ((), (), s32[]{:S(2)}) async-start(), calls=%async_computation.3 | async-start | bytes 2506752
  155.9 1.7 copy-start.12
  155.9 2.4 copy-start.16
  161.8 361.2 %copy-start.13 = (f32[1,64,384]{2,1,0:T(8,128)S(1)}, f32[1,64,384]{2,1,0:T(8,128)}, u32[]{:S(2)}) copy-start(f32[1,64,384]{2,1,0:T(8,128)} %param.19) | copy-start | bytes 294916
  161.8 361.2 %copy-start.14 = (f32[1,64,384]{2,1,0:T(8,128)S(1)}, f32[1,64,384]{2,1,0:T(8,128)}, u32[]{:S(2)}) copy-start(f32[1,64,384]{2,1,0:T(8,128)} %param.18) | copy-start | bytes 294916
  161.8 361.2 %copy-start.15 = (f32[1,64,384]{2,1,0:T(8,128)S(1)}, f32[1,64,384]{2,1,0:T(8,128)}, u32[]{:S(2)}) copy-start(f32[1,64,384]{2,1,0:T(8,128)} %param.17) | copy-start | bytes 294916
Sparse Core Ops, SparseCore 0:
  162.0 359.7 reduce-scatter.3
where the time goes:
time: 544 us; the launch traced here: 541 us
  waiting for transfers between devices  360 us (66%)
  blocking collectives  106 us (19%)
  local copies, waits for them, and re-layouts  35.6 us (7%)
  between operations  14.5 us (3%)
  matrix products  9.63 us (2%)
  starting transfers between devices  7.88 us (1%)
  other arithmetic  7.15 us (1%)
    unnamed x2, waiting for transfers between devices  360 us
    all_to_all x1, blocking collectives, in_one_piece(): lax.all_to_all(both, axis, split_axis=split_dim, concat_axis=concat_dim,...  106 us
  transfers between devices with their start and end apart: 2, of which 1 were waited for; matrix products, arithmetic and copies ran while one was open for 1% of the time, Pallas kernels for 0%

commit v1 on v0

v1 whole, which is shorter than its diff:
```python
import functools

import jax
import jax.numpy as jnp
from jax import lax
from jax.experimental import pallas as pl
from jax.experimental.pallas import tpu as pltpu
from jax.sharding import PartitionSpec as P

MESH = pl.DeviceIdType.MESH
F32 = jnp.float32
BF16 = jnp.bfloat16
CAP = 7
BLOCKS = 8

NN = (((1,), (0,)), ((), ()))
NT = (((1,), (1,)), ((), ()))
TN = (((0,), (0,)), ((), ()))


def dot(a, b, dims=NN):
    return lax.dot_general(a, b, dims, preferred_element_type=F32)


def iota(shape, dim):
    return lax.broadcasted_iota(jnp.int32, shape, dim)


def kernel(
    inner, replicas, topk,
    tok, ids, rw, og, wg, wu, wd, mg, mu, md,
    out_tok, out_route, out_g, out_u, out_d,
    snd, rcv, bsnd, brcv, pw, part, from_left, from_right,
    xs, gs, sc, gate, up, back, gg, gu, hid, slot, table,
    dsend, drecv, rsend, rrecv, wsend, wrecv, lsend, lrecv, gsend, grecv,
):
    tokens_here, width = tok.shape
    units = wg.shape[2]
    peers = rcv.shape[1] // 16
    experts = 2 * peers
    shard = width // replicas
    half_rows = width // 2
    wblock = half_rows // BLOCKS

    e = lax.axis_index("expert")
    r = lax.axis_index("replica")
    half = (e // inner) % 2
    me = (e // (2 * inner)) * inner + e % inner
    flip = inner * (1 - 2 * half)
    at_last = (r + 1) // replicas
    at_first = 1 - (r + replicas - 1) // replicas
    right = (e + at_last * flip, (r + 1) % replicas)
    left = (e + at_first * flip, (r + replicas - 1) % replicas)

    def peer(g):
        return ((g // inner) * 2 * inner + half * inner + g % inner, r)

    def ahead(i):
        return (me + i) % peers

    barrier = pltpu.get_barrier_semaphore()

    @pl.loop(1, peers)
    def _(i):
        pl.semaphore_signal(barrier, inc=1, device_id=peer(ahead(i)), device_id_type=MESH)

    for side in (left, right):
        pl.semaphore_signal(barrier, inc=1, device_id=side, device_id_type=MESH)

    eye = (iota((tokens_here, tokens_here), 0) == iota((tokens_here, tokens_here), 1)).astype(BF16)
    ids_t = dot(ids[...].astype(F32).astype(BF16), eye, TN)
    rw_t = dot(rw[...], eye, TN)
    row = iota((experts, 1), 0)
    group = row % peers
    order = (
        (group // inner) * 2 * inner + ((row // peers + half) % 2) * inner + group % inner
    ).astype(F32)
    named = jnp.zeros((experts, tokens_here), F32)
    weight_of = jnp.zeros((experts, tokens_here), F32)
    for k in range(topk):
        hit = ids_t[k : k + 1, :] == order
        named = jnp.where(hit, 1.0, named)
        weight_of = jnp.where(hit, rw_t[k : k + 1, :], weight_of)
    earlier = (iota((tokens_here, tokens_here), 0) < iota((tokens_here, tokens_here), 1)).astype(BF16)
    posm = jnp.where(named > 0.0, dot(named.astype(BF16), earlier), -1.0)
    table[...] = posm
    lane = iota((experts, 128), 1)
    slot_weight = jnp.zeros((experts, 128), F32)
    for j in range(CAP):
        w = jnp.sum(jnp.where(posm == float(j), weight_of, 0.0), axis=1, keepdims=True)
        slot_weight = jnp.where(lane == j, w, slot_weight)
    posm_b = posm.astype(BF16)
    slot_weight = slot_weight.astype(BF16)

    rows16 = 16 * peers
    rr = iota((rows16, experts), 0)
    ee = iota((rows16, experts), 1)
    pick_row = iota((rows16, 1), 0)
    for h in range(2):
        repeat = (ee == h * peers + rr // 16).astype(BF16)
        spread = dot(repeat, posm_b)
        chosen = spread == (pick_row % 8).astype(F32)
        upper = pick_row % 16 < 8
        from_tok = jnp.where(jnp.logical_and(chosen, upper), 1.0, 0.0).astype(BF16)
        from_og = jnp.where(jnp.logical_and(chosen, jnp.logical_not(upper)), 1.0, 0.0).astype(BF16)
        weights = jnp.where(pick_row % 16 == 7, dot(repeat, slot_weight), 0.0)
        step = width // 4 if width >= 512 else width // 2
        for c in range(0, width, step):
            block = dot(from_tok, tok[:, c : c + step]) + dot(from_og, og[:, c : c + step])
            if c == 0:
                snd[h, :, 0:128] = (block[:, 0:128] + weights).astype(BF16)
                snd[h, :, 128:step] = block[:, 128:].astype(BF16)
            else:
                snd[h, :, c : c + step] = block.astype(BF16)

    pl.semaphore_wait(barrier, peers + 1)

    def rows_of(g):
        return pl.ds(pl.multiple_of(g * 16, 16), 16)

    def dispatch(h, g, source):
        return pltpu.make_async_remote_copy(
            src_ref=snd.at[h, rows_of(g)],
            dst_ref=rcv.at[h, rows_of(source)],
            send_sem=dsend.at[h, g],
            recv_sem=drecv.at[h, source],
            device_id=peer(g),
            device_id_type=MESH,
        )

    def send_back(g, source):
        return pltpu.make_async_remote_copy(
            src_ref=bsnd.at[rows_of(g)],
            dst_ref=brcv.at[rows_of(source)],
            send_sem=rsend.at[g],
            recv_sem=rrecv.at[source],
            device_id=peer(g),
            device_id_type=MESH,
        )

    def weight_copy(d, m, b, source):
        rows = pl.ds(pl.multiple_of(d * half_rows + b * wblock, wblock), wblock)
        return pltpu.make_async_remote_copy(
            src_ref=source.at[0, rows] if source is not pw else pw.at[m, rows],
            dst_ref=pw.at[m, rows],
            send_sem=wsend.at[d, m * BLOCKS + b],
            recv_sem=wrecv.at[d, m * BLOCKS + b],
            device_id=right if d == 0 else left,
            device_id_type=MESH,
        )

    own = (wg, wu, wd)

    def pass_weights(m):
        @pl.loop(0, BLOCKS)
        def _(b):
            for d, edge in ((0, at_last), (1, at_first)):

                @pl.when(edge == 0)
                def _():
                    copy = weight_copy(d, m, b, pw)
                    copy.wait_recv()
                    copy.start()

    for m in range(3):
        for d, edge in ((0, at_last), (1, at_first)):

            @pl.when(edge == 1)
            def _():
                @pl.loop(0, BLOCKS)
                def _(b):
                    weight_copy(d, m, b, own[m]).start()

    for h in range(2):

        @pl.loop(1, peers)
        def _(i):
            dispatch(h, ahead(i), me).start()

        rcv[h, rows_of(me)] = snd[h, rows_of(me)]

    def expert(h, gate_w, up_w, down_w):
        @pl.loop(1, peers)
        def _(i):
            dispatch(h, me, ahead(i)).wait_recv()

        groups = min(4, peers)
        count = groups * 8

        @pl.loop(0, peers // groups)
        def _(i):
            block = rcv[h, pl.ds(pl.multiple_of(i * groups * 16, 16), groups * 16), :]
            block = block.astype(F32).reshape(groups, 2, 8, width)
            x, g = block[:, 0], block[:, 1]
            spread = jnp.broadcast_to(x[:, 7:8, 0:128], (groups, 8, 128)).reshape(count, 128)
            own_lane = iota((count, 128), 1) == iota((count, 128), 0) % 8
            own_lane = jnp.logical_and(own_lane, iota((count, 128), 1) < CAP)
            scale = jnp.sum(jnp.where(own_lane, spread, 0.0), axis=1, keepdims=True)
            x = x.reshape(count, width)
            g = g.reshape(count, width)
            x = jnp.where(iota((count, 1), 0) % 8 == 7, 0.0, x)
            at = pl.ds(pl.multiple_of(i * count, count), count)
            xs[at] = x.astype(BF16)
            gs[at] = g.astype(BF16)
            sc[at] = (scale * g).astype(BF16)
            slot[h, at, 0:128] = jnp.broadcast_to(scale, (count, 128))

        gate[...] = dot(xs[...], gate_w[...])
        up[...] = dot(xs[...], up_w[...])
        back[...] = dot(gs[...], down_w[...])

        @pl.loop(0, peers // groups)
        def _(i):
            at = pl.ds(pl.multiple_of(i * count, count), count)
            scale = slot[h, at, 0:128][:, 0:1]
            a, u, b = gate[at], up[at], back[at]
            sig = 1.0 / (1.0 + jnp.exp(-a))
            act = a * sig
            hidden = act * u
            route = jnp.sum(hidden * b, axis=1, keepdims=True)
            gh = scale * b
            gg[h, at] = (gh * u * sig * (1.0 + a * (1.0 - sig))).astype(BF16)
            gu[h, at] = (gh * act).astype(BF16)
            hid[at] = hidden.astype(BF16)
            slot[h, at, 128:256] = jnp.broadcast_to(route, (count, 128))

        depth = min(256, width)

        @pl.loop(0, width // depth)
        def _(i):
            at = pl.ds(pl.multiple_of(i * depth, depth), depth)
            x = xs[:, at]
            part[h, 0, at] = dot(x, gg[h], TN).astype(BF16)
            part[h, 1, at] = dot(x, gu[h], TN).astype(BF16)
            part[h, 2, at] = dot(sc[:, at], hid[...], TN).astype(BF16)

    def token_grads(h, gate_w, up_w):
        count = 8 * peers
        route = slot[h, :, 128:256]
        own_lane = iota((count, 128), 1) == iota((count, 128), 0) % 8
        own_lane = jnp.logical_and(own_lane, iota((count, 128), 1) < CAP)
        route = jnp.where(own_lane, route, 0.0).reshape(peers, 8, 128)
        route = jnp.broadcast_to(jnp.sum(route, axis=1, keepdims=True), (peers, 8, 128))
        route = jnp.where(iota((count, 128), 0) % 8 == 7, route.reshape(count, 128), 0.0)
        slot[h] = dot(gg[h], gate_w[...], NT) + dot(gu[h], up_w[...], NT)
        slot[h, :, 0:128] += route

    pass_weights(0)
    expert(0, wg.at[0], wu.at[0], wd.at[0])
    pass_weights(1)
    pass_weights(2)
    for m in range(3):
        for d, edge in ((0, at_last), (1, at_first)):

            @pl.when(edge == 1)
            def _():
                @pl.loop(0, BLOCKS)
                def _(b):
                    weight_copy(d, m, b, pw).wait_recv()

    expert(1, pw.at[0], pw.at[1], pw.at[2])

    z = half * replicas + r

    def shard_of(k):
        owner = (z + k) % (2 * replicas)
        rows = pl.ds(pl.multiple_of((owner % replicas) * shard, shard), shard)
        return (owner // replicas + half) % 2, rows

    def to_right(s, m, source):
        return pltpu.make_async_remote_copy(
            src_ref=source,
            dst_ref=from_left.at[s, m],
            send_sem=lsend.at[s * 3 + m],
            recv_sem=lrecv.at[s * 3 + m],
            device_id=right,
            device_id_type=MESH,
        )

    def to_left(s, m, source):
        return pltpu.make_async_remote_copy(
            src_ref=source,
            dst_ref=from_right.at[s, m],
            send_sem=gsend.at[s * 3 + m],
            recv_sem=grecv.at[s * 3 + m],
            device_id=left,
            device_id_type=MESH,
        )

    h_r, rows_r = shard_of(replicas)
    h_l, rows_l = shard_of(replicas + 1)
    for m in range(3):
        to_right(0, m, part.at[h_r, m, rows_r]).start()
        to_left(0, m, part.at[h_l, m, rows_l]).start()

    token_grads(0, wg.at[0], wu.at[0])
    token_grads(1, pw.at[0], pw.at[1])
    groups = min(4, peers)

    @pl.loop(0, peers // groups)
    def _(i):
        at = pl.ds(pl.multiple_of(i * groups * 8, groups * 8), groups * 8)
        a = slot[0, at].reshape(groups, 1, 8, width)
        b = slot[1, at].reshape(groups, 1, 8, width)
        both = jnp.concatenate([a, b], axis=1).reshape(groups * 16, width)
        bsnd[pl.ds(pl.multiple_of(i * groups * 16, 16), groups * 16)] = both.astype(BF16)

    @pl.loop(1, peers)
    def _(i):
        send_back(ahead(i), me).start()

    brcv[rows_of(me)] = bsnd[rows_of(me)]

    def add_right(s, m):
        h, rows = shard_of(replicas - 1 - s)
        to_right(s, m, from_left.at[s, m]).wait_recv()
        total = from_left[s, m].astype(F32) + part[h, m, rows].astype(F32)
        from_left[s, m] = total.astype(BF16)
        to_right(s + 1, m, from_left.at[s, m]).start()

    def add_left(s, m):
        h, rows = shard_of(replicas + 2 + s)
        to_left(s, m, from_right.at[s, m]).wait_recv()
        total = from_right[s, m].astype(F32) + part[h, m, rows].astype(F32)
        from_right[s, m] = total.astype(BF16)
        to_left(s + 1, m, from_right.at[s, m]).start()

    def ring(lo, hi):
        @pl.loop(lo, hi)
        def _(s):
            for m in range(3):
                add_right(s, m)
                add_left(s, m)

    middle = (replicas - 2) // 2
    ring(0, middle)

    @pl.loop(1, peers)
    def _(i):
        send_back(me, ahead(i)).wait_recv()

    posm = table[...]
    take = (ee == ((rr // 8) % 2) * peers + rr // 16).astype(BF16)
    chosen = dot(take, posm.astype(BF16)) == (pick_row % 8).astype(F32)
    chosen = jnp.where(chosen, 1.0, 0.0).astype(BF16)
    step = min(256, width)
    for c in range(0, width, step):
        out_tok[:, c : c + step] = dot(chosen, brcv[:, c : c + step], TN).astype(BF16)
    se = iota((experts, rows16), 0)
    sr = iota((experts, rows16), 1)
    last_row = (sr == (se % peers) * 16 + (se // peers) * 8 + 7).astype(BF16)
    routes = dot(last_row, brcv[:, 0:128])
    value = jnp.zeros((experts, tokens_here), F32)
    for j in range(CAP):
        value = jnp.where(posm == float(j), routes[:, j : j + 1], value)
    ids_t = dot(ids[...].astype(F32).astype(BF16), eye, TN)
    by_k = jnp.zeros((8, tokens_here), F32)
    for k in range(topk):
        mine = jnp.sum(jnp.where(ids_t[k : k + 1, :] == order, value, 0.0), axis=0, keepdims=True)
        by_k = jnp.where(iota((8, tokens_here), 0) == k, mine, by_k)
    out_route[...] = dot(eye, by_k.astype(BF16), NT)[:, 0:topk].astype(BF16)

    ring(middle, replicas - 2)
    for m in range(3):
        add_right(replicas - 2, m)
    h, rows = shard_of(0)
    for m, (mom, out) in enumerate(((mg, out_g), (mu, out_u), (md, out_d))):
        to_left(replicas - 2, m, from_right.at[replicas - 2, m]).wait_recv()
        to_right(replicas - 1, m, from_left.at[replicas - 1, m]).wait_recv()
        total = part[h, m, rows].astype(F32) + from_right[replicas - 2, m].astype(F32)
        total = total + from_left[replicas - 1, m].astype(F32)
        out[0] = 0.9 * mom[0] + 0.1 * total

    for h in range(2):

        @pl.loop(1, peers)
        def _(i):
            dispatch(h, ahead(i), me).wait_send()

    @pl.loop(1, peers)
    def _(i):
        send_back(ahead(i), me).wait_send()

    for m in range(3):

        @pl.loop(0, BLOCKS)
        def _(b):
            for d in range(2):
                weight_copy(d, m, b, pw).wait_send()

        @pl.loop(0, replicas)
        def _(s):
            to_right(s, m, from_left.at[s, m]).wait_send()

        @pl.loop(0, replicas - 1)
        def _(s):
            to_left(s, m, from_right.at[s, m]).wait_send()


def per_device(
    tokens, route_ids, route_weights, out_grad, w_gate, w_up, w_down, mom_gate, mom_up, mom_down
):
    groups = lax.axis_size("expert")
    replicas = lax.axis_size("replica")
    peers = groups // 2
    inner = 8 if groups == 64 else peers
    tok_rows, width = tokens.shape
    units = w_gate.shape[2]
    shard = width // replicas
    topk = route_ids.shape[1]
    deep = 8 * peers
    vmem = pltpu.VMEM
    dma = pltpu.SemaphoreType.DMA
    return pl.pallas_call(
        functools.partial(kernel, inner, replicas, topk),
        out_shape=(
            jax.ShapeDtypeStruct(tokens.shape, BF16),
            jax.ShapeDtypeStruct(route_ids.shape, BF16),
            jax.ShapeDtypeStruct(mom_gate.shape, F32),
            jax.ShapeDtypeStruct(mom_up.shape, F32),
            jax.ShapeDtypeStruct(mom_down.shape, F32),
        ),
        in_specs=[pl.BlockSpec(memory_space=vmem)] * 10,
        out_specs=[pl.BlockSpec(memory_space=vmem)] * 5,
        scratch_shapes=[
            vmem((2, 16 * peers, width), BF16),
            vmem((2, 16 * peers, width), BF16),
            vmem((16 * peers, width), BF16),
            vmem((16 * peers, width), BF16),
            vmem((3, width, units), BF16),
            vmem((2, 3, width, units), BF16),
            vmem((replicas, 3, shard, units), BF16),
            vmem((replicas - 1, 3, shard, units), BF16),
            vmem((deep, width), BF16),
            vmem((deep, width), BF16),
            vmem((deep, width), BF16),
            vmem((deep, units), F32),
            vmem((deep, units), F32),
            vmem((deep, units), F32),
            vmem((2, deep, units), BF16),
            vmem((2, deep, units), BF16),
            vmem((deep, units), BF16),
            vmem((2, deep, width), F32),
            vmem((groups, tok_rows), F32),
            dma((2, peers)),
            dma((2, peers)),
            dma((peers,)),
            dma((peers,)),
            dma((2, 3 * BLOCKS)),
            dma((2, 3 * BLOCKS)),
            dma((3 * replicas,)),
            dma((3 * replicas,)),
            dma((3 * (replicas - 1),)),
            dma((3 * (replicas - 1),)),
        ],
        compiler_params=pltpu.CompilerParams(
            collective_id=0, has_side_effects=True, vmem_limit_bytes=56 * 1024 * 1024
        ),
        cost_estimate=pl.CostEstimate(
            flops=2 * 2 * deep * width * units * 8, bytes_accessed=8 * 2**20, transcendentals=2 * deep * units
        ),
    )(tokens, route_ids, route_weights, out_grad, w_gate, w_up, w_down, mom_gate, mom_up, mom_down)


def solution(mesh):
    both = P(("expert", "replica"), None)
    held = P("expert", None, None)
    split = P("expert", "replica", None)
    return jax.shard_map(
        per_device,
        mesh=mesh,
        in_specs=(both,) * 4 + (held,) * 3 + (split,) * 3,
        out_specs=(both, both, split, split, split),
        check_vma=False,
    )
```

time: 544 us -> 2120 us (3.90)
  Pallas kernels: 0 us -> 2110 us
  waiting for transfers between devices: 360 us -> 0 us
  blocking collectives: 106 us -> 0 us
  local copies, waits for them, and re-layouts: 35.6 us -> 7.58 us
    pallas_call x0 -> x1, Pallas kernels: none -> 2110 us  [per_device(): pl.pallas_call(functools.partial(kernel, inner, replicas, topk), out_shap...]
    unnamed x2 -> x0, waiting for transfers between devices: 360 us -> none
    all_to_all x1 -> x0, blocking collectives: 106 us -> none  [in_one_piece(): lax.all_to_all(both, axis, split_axis=split_dim, concat_axis=concat_dim,...]
  transfers between devices with their start and end apart: 2 -> 0, of which waited for: 1 -> 0; matrix products, arithmetic and copies ran while one was open for 1% -> 0% of each run, Pallas kernels for 0% -> 0%
where the time goes in v1:
time: 2120 us
  Pallas kernels  2110 us (100%)
    pallas_call x1, Pallas kernels, per_device(): pl.pallas_call(functools.partial(kernel, inner, replicas, topk), out_shap...  2110 us

profile of v1, /device:TPU:6, one launch (start us, length us, event | category | flops | bytes accessed | tf_op | source)
XLA Modules:
  0.0 2123.1 jit_solution(17030617763361968248)
XLA Ops:
  0.6 0.0 copy-start.3
  0.6 1.4 copy.16.rw
  2.0 0.0 copy-done.3
  2.0 0.7 copy.15.ids
  2.7 2114.9 %shard_map.137 = (bf16[64,1024]{1,0:T(8,128)(2,1)}, bf16[64,6]{1,0:T(8,128)(2,1)}, f32[1,64,384]{2,1,0:T(8,128)}, f32[1,64,384]{2,1,0:T(8,128)}, f32[1,64,384]{2,1,0:T(8,128)}) custom-call(bf16[64,1024]{1,0:T(8,128)(2,1)} %tok.1, s32[64,6]{1,0:T(8,128)} %copy.15.ids, bf16[64,6]{1,0:T(8,128)(2,1)} %copy.16.rw, bf16[64,1024]{1,0:T(8,128)(2,1)} %og.1, ...), custom_call_target="tpu_custom_call" | custom-call | flops 3221225472 | bytes 8388608 | tf_op jit(solution)/shard_map/pallas_call | solution.py:414
  2117.6 1.4 copy.17
  2119.0 0.0 copy-start.2
  2119.0 1.6 copy.22
  2120.6 0.0 copy-done.2
  2120.6 0.0 copy-start.1
  2120.6 0.6 copy.23
  2121.3 0.3 copy-done.1
  2121.5 0.0 copy-start
  2121.5 0.6 copy.24
  2122.2 0.3 copy-done
  2122.5 0.6 copy.25
Async XLA Ops:
  0.6 1.4 copy-start.3
  2119.0 1.6 copy-start.2
  2120.6 0.9 copy-start.1
  2121.5 0.9 copy-start

commit v2 on v1

--- a/solution.py
+++ b/solution.py
@@ -11,7 +11,10 @@
 F32 = jnp.float32
 BF16 = jnp.bfloat16
 CAP = 7
-BLOCKS = 8
+BLOCKS = 32
+NEAR = 64
+LAG = 6
+OWN_AT = 50
 
 NN = (((1,), (0,)), ((), ()))
 NT = (((1,), (1,)), ((), ()))
@@ -39,8 +42,8 @@
     peers = rcv.shape[1] // 16
     experts = 2 * peers
     shard = width // replicas
-    half_rows = width // 2
-    wblock = half_rows // BLOCKS
+    wblock = width // BLOCKS
+    far = 3 * BLOCKS - NEAR
 
     e = lax.axis_index("expert")
     r = lax.axis_index("replica")
@@ -66,6 +69,85 @@
 
     for side in (left, right):
         pl.semaphore_signal(barrier, inc=1, device_id=side, device_id_type=MESH)
+
+    def rows_of(g):
+        return pl.ds(pl.multiple_of(g * 16, 16), 16)
+
+    def dispatch(h, g, source):
+        return pltpu.make_async_remote_copy(
+            src_ref=snd.at[h, rows_of(g)],
+            dst_ref=rcv.at[h, rows_of(source)],
+            send_sem=dsend.at[h, g],
+            recv_sem=drecv.at[h, source],
+            device_id=peer(g),
+            device_id_type=MESH,
+        )
+
+    def send_back(g, source):
+        return pltpu.make_async_remote_copy(
+            src_ref=bsnd.at[rows_of(g)],
+            dst_ref=brcv.at[rows_of(source)],
+            send_sem=rsend.at[g],
+            recv_sem=rrecv.at[source],
+            device_id=peer(g),
+            device_id_type=MESH,
+        )
+
+    def weight_copy(d, c, source):
+        q = c if d == 0 else 3 * BLOCKS - 1 - c
+        rows = pl.ds(pl.multiple_of((q % BLOCKS) * wblock, wblock), wblock)
+        landing = pw.at[q // BLOCKS, rows]
+        return pltpu.make_async_remote_copy(
+            src_ref=landing if source is None else source.at[0, rows],
+            dst_ref=landing,
+            send_sem=wsend.at[d, c],
+            recv_sem=wrecv.at[d, c],
+            device_id=right if d == 0 else left,
+            device_id_type=MESH,
+        )
+
+    place = (r, replicas - 1 - r)
+
+    def comes(d, c):
+        return jnp.logical_and(c >= 0, c < jnp.where(place[d] < replicas // 2, NEAR, far))
+
+    def goes_on(d, c):
+        sent = jnp.where(place[d] < replicas // 2 - 1, NEAR, jnp.where(place[d] < replicas - 1, far, 0))
+        return jnp.logical_and(c >= 0, c < sent)
+
+    def start_weights():
+        for d in range(2):
+
+            @pl.when(place[d] == replicas - 1)
+            def _():
+                for m, source in enumerate((wg, wu, wd)):
+                    first, last = m * BLOCKS, (m + 1) * BLOCKS
+                    if d == 1:
+                        first, last = 3 * BLOCKS - last, 3 * BLOCKS - first
+                    if first < NEAR:
+
+                        @pl.loop(first, min(last, NEAR))
+                        def _(c):
+                            weight_copy(d, c, source).start()
+
+    ticks = max(NEAR + LAG * (replicas // 2 - 1), far + LAG * (replicas - 1))
+
+    def pass_weights(lo, hi):
+        @pl.loop(lo, hi)
+        def _(t):
+            for d in range(2):
+                c = t - LAG * place[d]
+
+                @pl.when(comes(d, c))
+                def _():
+                    weight_copy(d, c, None).wait_recv()
+
+                @pl.when(goes_on(d, c))
+                def _():
+                    weight_copy(d, c, None).start()
+
+    pl.semaphore_wait(barrier, peers + 1)
+    start_weights()
 
     eye = (iota((tokens_here, tokens_here), 0) == iota((tokens_here, tokens_here), 1)).astype(BF16)
     ids_t = dot(ids[...].astype(F32).astype(BF16), eye, TN)
@@ -113,64 +195,6 @@
             else:
                 snd[h, :, c : c + step] = block.astype(BF16)
 
-    pl.semaphore_wait(barrier, peers + 1)
-
-    def rows_of(g):
-        return pl.ds(pl.multiple_of(g * 16, 16), 16)
-
-    def dispatch(h, g, source):
-        return pltpu.make_async_remote_copy(
-            src_ref=snd.at[h, rows_of(g)],
-            dst_ref=rcv.at[h, rows_of(source)],
-            send_sem=dsend.at[h, g],
-            recv_sem=drecv.at[h, source],
-            device_id=peer(g),
-            device_id_type=MESH,
-        )
-
-    def send_back(g, source):
-        return pltpu.make_async_remote_copy(
-            src_ref=bsnd.at[rows_of(g)],
-            dst_ref=brcv.at[rows_of(source)],
-            send_sem=rsend.at[g],
-            recv_sem=rrecv.at[source],
-            device_id=peer(g),
-            device_id_type=MESH,
-        )
-
-    def weight_copy(d, m, b, source):
-        rows = pl.ds(pl.multiple_of(d * half_rows + b * wblock, wblock), wblock)
-        return pltpu.make_async_remote_copy(
-            src_ref=source.at[0, rows] if source is not pw else pw.at[m, rows],
-            dst_ref=pw.at[m, rows],
-            send_sem=wsend.at[d, m * BLOCKS + b],
-            recv_sem=wrecv.at[d, m * BLOCKS + b],
-            device_id=right if d == 0 else left,
-            device_id_type=MESH,
-        )
-
-    own = (wg, wu, wd)
-
-    def pass_weights(m):
-        @pl.loop(0, BLOCKS)
-        def _(b):
-            for d, edge in ((0, at_last), (1, at_first)):
-
-                @pl.when(edge == 0)
-                def _():
-                    copy = weight_copy(d, m, b, pw)
-                    copy.wait_recv()
-                    copy.start()
-
-    for m in range(3):
-        for d, edge in ((0, at_last), (1, at_first)):
-
-            @pl.when(edge == 1)
-            def _():
-                @pl.loop(0, BLOCKS)
-                def _(b):
-                    weight_copy(d, m, b, own[m]).start()
-
     for h in range(2):
 
         @pl.loop(1, peers)
@@ -245,19 +269,9 @@
         slot[h] = dot(gg[h], gate_w[...], NT) + dot(gu[h], up_w[...], NT)
         slot[h, :, 0:128] += route
 
-    pass_weights(0)
+    pass_weights(0, min(OWN_AT, ticks))
     expert(0, wg.at[0], wu.at[0], wd.at[0])
-    pass_weights(1)
-    pass_weights(2)
-    for m in range(3):
-        for d, edge in ((0, at_last), (1, at_first)):
-
-            @pl.when(edge == 1)
-            def _():
-                @pl.loop(0, BLOCKS)
-                def _(b):
-                    weight_copy(d, m, b, pw).wait_recv()
-
+    pass_weights(min(OWN_AT, ticks), ticks)
     expert(1, pw.at[0], pw.at[1], pw.at[2])
 
     z = half * replicas + r
@@ -381,12 +395,15 @@
     def _(i):
         send_back(ahead(i), me).wait_send()
 
+    @pl.loop(0, NEAR)
+    def _(c):
+        for d in range(2):
+
+            @pl.when(jnp.logical_or(place[d] == replicas - 1, goes_on(d, c)))
+            def _():
+                weight_copy(d, c, None).wait_send()
+
     for m in range(3):
-
-        @pl.loop(0, BLOCKS)
-        def _(b):
-            for d in range(2):
-                weight_copy(d, m, b, pw).wait_send()
 
         @pl.loop(0, replicas)
         def _(s):
@@ -446,8 +463,8 @@
             dma((2, peers)),
             dma((peers,)),
             dma((peers,)),
-            dma((2, 3 * BLOCKS)),
-            dma((2, 3 * BLOCKS)),
+            dma((2, NEAR)),
+            dma((2, NEAR)),
             dma((3 * replicas,)),
             dma((3 * replicas,)),
             dma((3 * (replicas - 1),)),

time: 2120 us -> 192 us (0.09)
  Pallas kernels: 2110 us -> 182 us
    pallas_call x1, Pallas kernels: 2110 us -> 182 us  [per_device(): pl.pallas_call(functools.partial(kernel, inner, replicas, topk), out_shap...]
where the time goes in v2:
time: 192 us; the launch traced here: 190 us
  Pallas kernels  182 us (95%)
  local copies, waits for them, and re-layouts  7.58 us (4%)
    pallas_call x1, Pallas kernels, per_device(): pl.pallas_call(functools.partial(kernel, inner, replicas, topk), out_shap...  182 us
    unnamed x14, local copies, waits for them, and re-layouts  6.2 us

profile of v2, /device:TPU:6, one launch (start us, length us, event | category | flops | bytes accessed | tf_op | source)
XLA Modules:
  0.0 189.8 jit_solution(12974127650638195281)
XLA Ops:
  0.6 0.0 copy-start.3
  0.6 1.4 copy.16.rw
  2.0 0.0 copy-done.3
  2.0 0.7 copy.15.ids
  2.7 181.6 %shard_map.137 = (bf16[64,1024]{1,0:T(8,128)(2,1)}, bf16[64,6]{1,0:T(8,128)(2,1)}, f32[1,64,384]{2,1,0:T(8,128)}, f32[1,64,384]{2,1,0:T(8,128)}, f32[1,64,384]{2,1,0:T(8,128)}) custom-call(bf16[64,1024]{1,0:T(8,128)(2,1)} %tok.1, s32[64,6]{1,0:T(8,128)} %copy.15.ids, bf16[64,6]{1,0:T(8,128)(2,1)} %copy.16.rw, bf16[64,1024]{1,0:T(8,128)(2,1)} %og.1, ...), custom_call_target="tpu_custom_call" | custom-call | flops 3221225472 | bytes 8388608 | tf_op jit(solution)/shard_map/pallas_call | solution.py:431
  184.3 1.4 copy.17
  185.7 0.0 copy-start.2
  185.7 1.6 copy.22
  187.3 0.0 copy-done.2
  187.3 0.0 copy-start.1
  187.3 0.6 copy.23
  187.9 0.3 copy-done.1
  188.2 0.0 copy-start
  188.2 0.6 copy.24
  188.9 0.3 copy-done
  189.2 0.6 copy.25
Async XLA Ops:
  0.6 1.4 copy-start.3
  185.7 1.6 copy-start.2
  187.3 0.9 copy-start.1
  188.2 0.9 copy-start

commit v3 on v2

--- a/solution.py
+++ b/solution.py
@@ -12,9 +12,10 @@
 BF16 = jnp.bfloat16
 CAP = 7
 BLOCKS = 32
-NEAR = 64
 LAG = 6
-OWN_AT = 50
+PIECES = 6
+OWN_AT = 28
+RETURNED_AT = 9
 
 NN = (((1,), (0,)), ((), ()))
 NT = (((1,), (1,)), ((), ()))
@@ -34,7 +35,7 @@
     tok, ids, rw, og, wg, wu, wd, mg, mu, md,
     out_tok, out_route, out_g, out_u, out_d,
     snd, rcv, bsnd, brcv, pw, part, from_left, from_right,
-    xs, gs, sc, gate, up, back, gg, gu, hid, slot, table,
+    xs, gs, sc, gate, up, back, gg, gu, hid, scales, routes, slot, table,
     dsend, drecv, rsend, rrecv, wsend, wrecv, lsend, lrecv, gsend, grecv,
 ):
     tokens_here, width = tok.shape
@@ -43,7 +44,10 @@
     experts = 2 * peers
     shard = width // replicas
     wblock = width // BLOCKS
-    far = 3 * BLOCKS - NEAR
+    groups = min(4, peers)
+    count = groups * 8
+    deep = 8 * peers
+    quarters = 4 if peers >= 32 else 1
 
     e = lax.axis_index("expert")
     r = lax.axis_index("replica")
@@ -108,12 +112,15 @@
 
     place = (r, replicas - 1 - r)
 
+    def reach(p):
+        return 3 * BLOCKS // 2 + (replicas - 1 - 2 * p) * (LAG // 2)
+
     def comes(d, c):
-        return jnp.logical_and(c >= 0, c < jnp.where(place[d] < replicas // 2, NEAR, far))
+        return jnp.logical_and(c >= 0, c < reach(place[d]))
 
     def goes_on(d, c):
-        sent = jnp.where(place[d] < replicas // 2 - 1, NEAR, jnp.where(place[d] < replicas - 1, far, 0))
-        return jnp.logical_and(c >= 0, c < sent)
+        more = jnp.logical_and(place[d] < replicas - 1, c < reach(place[d] + 1))
+        return jnp.logical_and(c >= 0, more)
 
     def start_weights():
         for d in range(2):
@@ -124,15 +131,15 @@
                     first, last = m * BLOCKS, (m + 1) * BLOCKS
                     if d == 1:
                         first, last = 3 * BLOCKS - last, 3 * BLOCKS - first
-                    if first < NEAR:
-
-                        @pl.loop(first, min(last, NEAR))
+                    if first < reach(0):
+
+                        @pl.loop(first, min(last, reach(0)))
                         def _(c):
                             weight_copy(d, c, source).start()
 
-    ticks = max(NEAR + LAG * (replicas // 2 - 1), far + LAG * (replicas - 1))
-
-    def pass_weights(lo, hi):
+    ticks = reach(0)
+
+    def pass_weights(lo, hi, work=None):
         @pl.loop(lo, hi)
         def _(t):
             for d in range(2):
@@ -146,12 +153,14 @@
                 def _():
                     weight_copy(d, c, None).start()
 
+            if work is not None:
+                work(t - lo)
+
     pl.semaphore_wait(barrier, peers + 1)
     start_weights()
 
-    eye = (iota((tokens_here, tokens_here), 0) == iota((tokens_here, tokens_here), 1)).astype(BF16)
-    ids_t = dot(ids[...].astype(F32).astype(BF16), eye, TN)
-    rw_t = dot(rw[...], eye, TN)
+    ids_t = ids[...].astype(F32)
+    rw_t = rw[...].astype(F32)
     row = iota((experts, 1), 0)
     group = row % peers
     order = (
@@ -188,6 +197,8 @@
         weights = jnp.where(pick_row % 16 == 7, dot(repeat, slot_weight), 0.0)
         step = width // 4 if width >= 512 else width // 2
         for c in range(0, width, step):
+            tick = h * (width // step) + c // step
+            pass_weights(tick, tick + 1)
             block = dot(from_tok, tok[:, c : c + step]) + dot(from_og, og[:, c : c + step])
             if c == 0:
                 snd[h, :, 0:128] = (block[:, 0:128] + weights).astype(BF16)
@@ -195,24 +206,20 @@
             else:
                 snd[h, :, c : c + step] = block.astype(BF16)
 
-    for h in range(2):
-
         @pl.loop(1, peers)
         def _(i):
             dispatch(h, ahead(i), me).start()
 
         rcv[h, rows_of(me)] = snd[h, rows_of(me)]
 
-    def expert(h, gate_w, up_w, down_w):
+
+    def received(h):
         @pl.loop(1, peers)
         def _(i):
             dispatch(h, me, ahead(i)).wait_recv()
 
-        groups = min(4, peers)
-        count = groups * 8
-
-        @pl.loop(0, peers // groups)
-        def _(i):
+    def unpack(h):
+        def some(i):
             block = rcv[h, pl.ds(pl.multiple_of(i * groups * 16, 16), groups * 16), :]
             block = block.astype(F32).reshape(groups, 2, 8, width)
             x, g = block[:, 0], block[:, 1]
@@ -224,19 +231,26 @@
             g = g.reshape(count, width)
             x = jnp.where(iota((count, 1), 0) % 8 == 7, 0.0, x)
             at = pl.ds(pl.multiple_of(i * count, count), count)
-            xs[at] = x.astype(BF16)
-            gs[at] = g.astype(BF16)
-            sc[at] = (scale * g).astype(BF16)
-            slot[h, at, 0:128] = jnp.broadcast_to(scale, (count, 128))
-
-        gate[...] = dot(xs[...], gate_w[...])
-        up[...] = dot(xs[...], up_w[...])
-        back[...] = dot(gs[...], down_w[...])
-
-        @pl.loop(0, peers // groups)
-        def _(i):
+            xs[h, at] = x.astype(BF16)
+            gs[h, at] = g.astype(BF16)
+            sc[h, at] = (scale * g).astype(BF16)
+            scales[h, at] = jnp.broadcast_to(scale, (count, 128))
+
+        return some
+
+    def expert(h, gate_w, up_w, down_w):
+        def gates(i):
+            gate[...] = dot(xs[h], gate_w[...])
+
+        def ups(i):
+            up[...] = dot(xs[h], up_w[...])
+
+        def backs(i):
+            back[...] = dot(gs[h], down_w[...])
+
+        def products(i):
             at = pl.ds(pl.multiple_of(i * count, count), count)
-            scale = slot[h, at, 0:128][:, 0:1]
+            scale = scales[h, at][:, 0:1]
             a, u, b = gate[at], up[at], back[at]
             sig = 1.0 / (1.0 + jnp.exp(-a))
             act = a * sig
@@ -246,47 +260,64 @@
             gg[h, at] = (gh * u * sig * (1.0 + a * (1.0 - sig))).astype(BF16)
             gu[h, at] = (gh * act).astype(BF16)
             hid[at] = hidden.astype(BF16)
-            slot[h, at, 128:256] = jnp.broadcast_to(route, (count, 128))
+            routes[h, at] = jnp.broadcast_to(route, (count, 128))
 
         depth = min(256, width)
 
-        @pl.loop(0, width // depth)
-        def _(i):
+        def parts(i):
             at = pl.ds(pl.multiple_of(i * depth, depth), depth)
-            x = xs[:, at]
+            x = xs[h, :, at]
             part[h, 0, at] = dot(x, gg[h], TN).astype(BF16)
             part[h, 1, at] = dot(x, gu[h], TN).astype(BF16)
-            part[h, 2, at] = dot(sc[:, at], hid[...], TN).astype(BF16)
-
-    def token_grads(h, gate_w, up_w):
-        count = 8 * peers
-        route = slot[h, :, 128:256]
-        own_lane = iota((count, 128), 1) == iota((count, 128), 0) % 8
-        own_lane = jnp.logical_and(own_lane, iota((count, 128), 1) < CAP)
-        route = jnp.where(own_lane, route, 0.0).reshape(peers, 8, 128)
-        route = jnp.broadcast_to(jnp.sum(route, axis=1, keepdims=True), (peers, 8, 128))
-        route = jnp.where(iota((count, 128), 0) % 8 == 7, route.reshape(count, 128), 0.0)
-        slot[h] = dot(gg[h], gate_w[...], NT) + dot(gu[h], up_w[...], NT)
-        slot[h, :, 0:128] += route
-
-    pass_weights(0, min(OWN_AT, ticks))
-    expert(0, wg.at[0], wu.at[0], wd.at[0])
-    pass_weights(min(OWN_AT, ticks), ticks)
-    expert(1, pw.at[0], pw.at[1], pw.at[2])
+            part[h, 2, at] = dot(sc[h, :, at], hid[...], TN).astype(BF16)
+
+        turns, blocks = peers // groups, width // depth
+        return ((gates, 1), (ups, 1), (backs, 1), (products, turns), (parts, blocks))
+
+    def token_grads(h, at, rows, gate_w, up_w):
+        own_lane = iota((rows, 128), 1) == iota((rows, 128), 0) % 8
+        own_lane = jnp.logical_and(own_lane, iota((rows, 128), 1) < CAP)
+        route = jnp.where(own_lane, routes[h, at], 0.0).reshape(rows // 8, 8, 128)
+        route = jnp.broadcast_to(jnp.sum(route, axis=1, keepdims=True), (rows // 8, 8, 128))
+        route = jnp.where(iota((rows, 128), 0) % 8 == 7, route.reshape(rows, 128), 0.0)
+        slot[h, at] = dot(gg[h, at], gate_w[...], NT) + dot(gu[h, at], up_w[...], NT)
+        slot[h, at, 0:128] += route
+
+    def own_quarter(i):
+        rows = deep // quarters
+        at = pl.ds(pl.multiple_of(i * rows, rows), rows)
+        token_grads(0, at, rows, wg.at[0], wu.at[0])
+
+    turns = peers // groups
+    tick = 2 * (width // step)
+    pass_weights(tick, OWN_AT)
+    tick = OWN_AT
+    received(0)
+    stages = ((unpack(0), turns),) + expert(0, wg.at[0], wu.at[0], wd.at[0]) + ((own_quarter, quarters),)
+    for work, times in stages:
+        pass_weights(tick, tick + times, work)
+        tick += times
+    received(1)
+    pass_weights(tick, tick + turns, unpack(1))
+    pass_weights(tick + turns, max(ticks, tick + turns))
+    for work, times in expert(1, pw.at[0], pw.at[1], pw.at[2]):
+        pl.loop(0, times)(work)
 
     z = half * replicas + r
 
-    def shard_of(k):
+    def shard_of(k, m):
         owner = (z + k) % (2 * replicas)
-        rows = pl.ds(pl.multiple_of((owner % replicas) * shard, shard), shard)
-        return (owner // replicas + half) % 2, rows
+        piece = 3 * shard // PIECES
+        first = (owner % replicas) * shard + (m % (PIECES // 3)) * piece
+        rows = pl.ds(pl.multiple_of(first, piece), piece)
+        return (owner // replicas + half) % 2, m // (PIECES // 3), rows
 
     def to_right(s, m, source):
         return pltpu.make_async_remote_copy(
             src_ref=source,
             dst_ref=from_left.at[s, m],
-            send_sem=lsend.at[s * 3 + m],
-            recv_sem=lrecv.at[s * 3 + m],
+            send_sem=lsend.at[s * PIECES + m],
+            recv_sem=lrecv.at[s * PIECES + m],
             device_id=right,
             device_id_type=MESH,
         )
@@ -295,59 +326,64 @@
         return pltpu.make_async_remote_copy(
             src_ref=source,
             dst_ref=from_right.at[s, m],
-            send_sem=gsend.at[s * 3 + m],
-            recv_sem=grecv.at[s * 3 + m],
+            send_sem=gsend.at[s * PIECES + m],
+            recv_sem=grecv.at[s * PIECES + m],
             device_id=left,
             device_id_type=MESH,
         )
 
-    h_r, rows_r = shard_of(replicas)
-    h_l, rows_l = shard_of(replicas + 1)
-    for m in range(3):
-        to_right(0, m, part.at[h_r, m, rows_r]).start()
-        to_left(0, m, part.at[h_l, m, rows_l]).start()
-
-    token_grads(0, wg.at[0], wu.at[0])
-    token_grads(1, pw.at[0], pw.at[1])
-    groups = min(4, peers)
-
-    @pl.loop(0, peers // groups)
-    def _(i):
-        at = pl.ds(pl.multiple_of(i * groups * 8, groups * 8), groups * 8)
-        a = slot[0, at].reshape(groups, 1, 8, width)
-        b = slot[1, at].reshape(groups, 1, 8, width)
-        both = jnp.concatenate([a, b], axis=1).reshape(groups * 16, width)
-        bsnd[pl.ds(pl.multiple_of(i * groups * 16, 16), groups * 16)] = both.astype(BF16)
-
-    @pl.loop(1, peers)
-    def _(i):
-        send_back(ahead(i), me).start()
-
-    brcv[rows_of(me)] = bsnd[rows_of(me)]
+    for m in range(PIECES):
+        to_right(0, m, part.at[shard_of(replicas, m)]).start()
+        to_left(0, m, part.at[shard_of(replicas + 1, m)]).start()
+
+    def return_some(i):
+        rows = deep // quarters
+        quarter = (me * quarters // peers + i) % quarters
+        at = pl.ds(pl.multiple_of(quarter * rows, rows), rows)
+        token_grads(1, at, rows, pw.at[0], pw.at[1])
+        a = slot[0, at].reshape(rows // 8, 1, 8, width)
+        b = slot[1, at].reshape(rows // 8, 1, 8, width)
+        blocks = jnp.concatenate([a, b], axis=1).reshape(rows * 2, width)
+        bsnd[pl.ds(pl.multiple_of(quarter * rows * 2, rows * 2), rows * 2)] = blocks.astype(BF16)
+        some = peers // quarters
+
+        @pl.loop(0, some)
+        def _(j):
+            g = quarter * some + (me + j) % some
+
+            @pl.when(g != me)
+            def _():
+                send_back(g, me).start()
+
+            @pl.when(g == me)
+            def _():
+                brcv[rows_of(me)] = bsnd[rows_of(me)]
 
     def add_right(s, m):
-        h, rows = shard_of(replicas - 1 - s)
+        h, w, rows = shard_of(replicas - 1 - s, m)
         to_right(s, m, from_left.at[s, m]).wait_recv()
-        total = from_left[s, m].astype(F32) + part[h, m, rows].astype(F32)
+        total = from_left[s, m].astype(F32) + part[h, w, rows].astype(F32)
         from_left[s, m] = total.astype(BF16)
         to_right(s + 1, m, from_left.at[s, m]).start()
 
     def add_left(s, m):
-        h, rows = shard_of(replicas + 2 + s)
+        h, w, rows = shard_of(replicas + 2 + s, m)
         to_left(s, m, from_right.at[s, m]).wait_recv()
-        total = from_right[s, m].astype(F32) + part[h, m, rows].astype(F32)
+        total = from_right[s, m].astype(F32) + part[h, w, rows].astype(F32)
         from_right[s, m] = total.astype(BF16)
         to_left(s + 1, m, from_right.at[s, m]).start()
 
-    def ring(lo, hi):
-        @pl.loop(lo, hi)
+    def ring(lo, hi, work=None):
+        @pl.loop(min(lo, replicas - 2), min(hi, replicas - 2))
         def _(s):
-            for m in range(3):
+            for m in range(PIECES):
                 add_right(s, m)
                 add_left(s, m)
-
-    middle = (replicas - 2) // 2
-    ring(0, middle)
+            if work is not None:
+                work(s - lo)
+
+    ring(0, quarters, return_some)
+    ring(quarters, RETURNED_AT)
 
     @pl.loop(1, peers)
     def _(i):
@@ -360,30 +396,34 @@
     step = min(256, width)
     for c in range(0, width, step):
         out_tok[:, c : c + step] = dot(chosen, brcv[:, c : c + step], TN).astype(BF16)
+    ring(RETURNED_AT, RETURNED_AT + 1)
     se = iota((experts, rows16), 0)
     sr = iota((experts, rows16), 1)
     last_row = (sr == (se % peers) * 16 + (se // peers) * 8 + 7).astype(BF16)
-    routes = dot(last_row, brcv[:, 0:128])
+    returned = dot(last_row, brcv[:, 0:128])
     value = jnp.zeros((experts, tokens_here), F32)
     for j in range(CAP):
-        value = jnp.where(posm == float(j), routes[:, j : j + 1], value)
-    ids_t = dot(ids[...].astype(F32).astype(BF16), eye, TN)
+        value = jnp.where(posm == float(j), returned[:, j : j + 1], value)
+    ids_t = ids[...].astype(F32)
     by_k = jnp.zeros((8, tokens_here), F32)
     for k in range(topk):
         mine = jnp.sum(jnp.where(ids_t[k : k + 1, :] == order, value, 0.0), axis=0, keepdims=True)
         by_k = jnp.where(iota((8, tokens_here), 0) == k, mine, by_k)
-    out_route[...] = dot(eye, by_k.astype(BF16), NT)[:, 0:topk].astype(BF16)
-
-    ring(middle, replicas - 2)
-    for m in range(3):
+    out_route[...] = by_k[0:topk].astype(BF16)
+
+    ring(RETURNED_AT + 1, replicas - 2)
+    for m in range(PIECES):
         add_right(replicas - 2, m)
-    h, rows = shard_of(0)
-    for m, (mom, out) in enumerate(((mg, out_g), (mu, out_u), (md, out_d))):
+    piece = 3 * shard // PIECES
+    moms, outs = (mg, mu, md), (out_g, out_u, out_d)
+    for m in range(PIECES):
+        h, w, rows = shard_of(0, m)
         to_left(replicas - 2, m, from_right.at[replicas - 2, m]).wait_recv()
         to_right(replicas - 1, m, from_left.at[replicas - 1, m]).wait_recv()
-        total = part[h, m, rows].astype(F32) + from_right[replicas - 2, m].astype(F32)
+        total = part[h, w, rows].astype(F32) + from_right[replicas - 2, m].astype(F32)
         total = total + from_left[replicas - 1, m].astype(F32)
-        out[0] = 0.9 * mom[0] + 0.1 * total
+        at = pl.ds((m % (PIECES // 3)) * piece, piece)
+        outs[w][0, at] = 0.9 * moms[w][0, at] + 0.1 * total
 
     for h in range(2):
 
@@ -395,7 +435,7 @@
     def _(i):
         send_back(ahead(i), me).wait_send()
 
-    @pl.loop(0, NEAR)
+    @pl.loop(0, ticks)
     def _(c):
         for d in range(2):
 
@@ -403,7 +443,7 @@
             def _():
                 weight_copy(d, c, None).wait_send()
 
-    for m in range(3):
+    for m in range(PIECES):
 
         @pl.loop(0, replicas)
         def _(s):
@@ -428,11 +468,11 @@
     deep = 8 * peers
     vmem = pltpu.VMEM
     dma = pltpu.SemaphoreType.DMA
-    return pl.pallas_call(
+    outs = pl.pallas_call(
         functools.partial(kernel, inner, replicas, topk),
         out_shape=(
             jax.ShapeDtypeStruct(tokens.shape, BF16),
-            jax.ShapeDtypeStruct(route_ids.shape, BF16),
+            jax.ShapeDtypeStruct((topk, tok_rows), BF16),
             jax.ShapeDtypeStruct(mom_gate.shape, F32),
             jax.ShapeDtypeStruct(mom_up.shape, F32),
             jax.ShapeDtypeStruct(mom_down.shape, F32),
@@ -446,29 +486,31 @@
             vmem((16 * peers, width), BF16),
             vmem((3, width, units), BF16),
             vmem((2, 3, width, units), BF16),
-            vmem((replicas, 3, shard, units), BF16),
-            vmem((replicas - 1, 3, shard, units), BF16),
-            vmem((deep, width), BF16),
-            vmem((deep, width), BF16),
-            vmem((deep, width), BF16),
+            vmem((replicas, PIECES, 3 * shard // PIECES, units), BF16),
+            vmem((replicas - 1, PIECES, 3 * shard // PIECES, units), BF16),
+            vmem((2, deep, width), BF16),
+            vmem((2, deep, width), BF16),
+            vmem((2, deep, width), BF16),
             vmem((deep, units), F32),
             vmem((deep, units), F32),
             vmem((deep, units), F32),
             vmem((2, deep, units), BF16),
             vmem((2, deep, units), BF16),
             vmem((deep, units), BF16),
+            vmem((2, deep, 128), F32),
+            vmem((2, deep, 128), F32),
             vmem((2, deep, width), F32),
             vmem((groups, tok_rows), F32),
             dma((2, peers)),
             dma((2, peers)),
             dma((peers,)),
             dma((peers,)),
-            dma((2, NEAR)),
-            dma((2, NEAR)),
-            dma((3 * replicas,)),
-            dma((3 * replicas,)),
-            dma((3 * (replicas - 1),)),
-            dma((3 * (replicas - 1),)),
+            dma((2, 3 * BLOCKS)),
+            dma((2, 3 * BLOCKS)),
+            dma((PIECES * replicas,)),
+            dma((PIECES * replicas,)),
+            dma((PIECES * (replicas - 1),)),
+            dma((PIECES * (replicas - 1),)),
         ],
         compiler_params=pltpu.CompilerParams(
             collective_id=0, has_side_effects=True, vmem_limit_bytes=56 * 1024 * 1024
@@ -476,7 +518,8 @@
         cost_estimate=pl.CostEstimate(
             flops=2 * 2 * deep * width * units * 8, bytes_accessed=8 * 2**20, transcendentals=2 * deep * units
         ),
-    )(tokens, route_ids, route_weights, out_grad, w_gate, w_up, w_down, mom_gate, mom_up, mom_down)
+    )(tokens, route_ids.T, route_weights.T, out_grad, w_gate, w_up, w_down, mom_gate, mom_up, mom_down)
+    return (outs[0], outs[1].T, *outs[2:])
 
 
 def solution(mesh):

time: 192 us -> 190 us (0.990); the launches traced: 190 us -> 190 us
  Pallas kernels: 182 us -> 185 us
  local copies, waits for them, and re-layouts: 7.58 us -> 4.68 us
    pallas_call x1, Pallas kernels: 182 us -> 185 us  [per_device(): pl.pallas_call(functools.partial(kernel, inner, replicas, topk), out_shap...]
    unnamed x14 -> x13, local copies, waits for them, and re-layouts: 6.2 us -> 4.68 us
where the time goes in v3:
time: 190 us
  Pallas kernels  185 us (97%)
  local copies, waits for them, and re-layouts  4.68 us (2%)
    pallas_call x1, Pallas kernels, per_device(): pl.pallas_call(functools.partial(kernel, inner, replicas, topk), out_shap...  185 us
    unnamed x13, local copies, waits for them, and re-layouts  4.68 us

profile of v3, /device:TPU:6, one launch (start us, length us, event | category | flops | bytes accessed | tf_op | source)
XLA Modules:
  0.0 189.9 jit_solution(13115053310477206553)
XLA Ops:
  0.6 184.6 %shard_map.137 = (bf16[64,1024]{1,0:T(8,128)(2,1)}, bf16[6,64]{1,0:T(8,128)(2,1)}, f32[1,64,384]{2,1,0:T(8,128)}, f32[1,64,384]{2,1,0:T(8,128)}, f32[1,64,384]{2,1,0:T(8,128)}) custom-call(bf16[64,1024]{1,0:T(8,128)(2,1)} %tok.1, s32[6,64]{1,0:T(8,128)} %bitcast.4, bf16[6,64]{1,0:T(8,128)(2,1)} %bitcast.5, bf16[64,1024]{1,0:T(8,128)(2,1)} %og.1, ...), custom_call_target="tpu_custom_call" | custom-call | flops 3221225472 | bytes 8388608 | tf_op jit(solution)/shard_map/pallas_call | solution.py:471
  185.2 0.0 copy-start.3
  185.2 0.0 copy-start.2
  185.2 1.6 copy.20
  186.9 0.0 copy-done.3
  186.9 0.6 copy.21
  187.4 0.0 copy-done.2
  187.4 0.0 copy-start.1
  187.4 0.6 copy.22
  188.1 0.3 copy-done.1
  188.4 0.0 copy-start
  188.4 0.6 copy.23
  189.0 0.3 copy-done
  189.3 0.6 copy.24
Async XLA Ops:
  185.2 1.6 copy-start.3
  185.2 2.2 %copy-start.2 = (f32[1,64,384]{2,1,0:T(8,128)S(1)}, f32[1,64,384]{2,1,0:T(8,128)}, u32[]{:S(2)}) copy-start(f32[1,64,384]{2,1,0:T(8,128)} %get-tuple-element.22) | copy-start | bytes 294916
  187.4 0.9 copy-start.1
  188.4 0.9 copy-start
